TPU v7x, 32 devices: a whole 2x2x4 slice. The times are simulated.
32 devices in a mesh: dp: 4 (over x, core), sp: 8 (over z, y).
Axes of the slice: x: 2, y: 2, z: 4, core: 2. Of those that a mesh axis runs over, the one named last changes fastest.
Arguments:
- frames_in: bfloat16 [2048, 64, 256], P(('dp', 'sp')), may hold values from -6 to 6
- spatial_weight: bfloat16 [3, 3, 256, 256], replicated, may hold values from -0.125 to 0.125
- temporal_weight: bfloat16 [3, 256, 256], replicated, may hold values from -0.21875 to 0.21875
- cotangent: bfloat16 [2048, 64, 256], P(('dp', 'sp')), may hold values from -6 to 6
Outputs:
- block_out: bfloat16 [2048, 64, 256], P(('dp', 'sp'))
- grad_input: bfloat16 [2048, 64, 256], P(('dp', 'sp'))
- grad_spatial: float32 [3, 3, 256, 256], replicated
- grad_temporal: float32 [3, 256, 256], replicated
All inputs are finite; a program needn't handle non-finite values.
Results may differ from a plain program's by a relative error of at most 0.0049.
Values may be sent and summed in bfloat16 or wider, within the bound.
A program may use at most 128 MiB of HBM per device.

v0:
```python
import math
import jax
import jax.numpy as jnp
from jax import lax
from jax.sharding import PartitionSpec as P

H = 64
FRAMES = 4


def contract_rows(left, right):
    return lax.dot_general(
        left, right, (((0,), (0,)), ((), ())), preferred_element_type=jnp.float32
    )


def times_transpose(left, weight):
    return lax.dot_general(
        left, weight, (((1,), (1,)), ((), ())), preferred_element_type=jnp.float32
    )


def local(frames_in, spatial_weight, temporal_weight, cotangent):
    slab_rows, width_cells, channels = frames_in.shape
    sp_count = lax.axis_size("sp")

    def padded_rows(values):
        return jnp.pad(values, ((1, 1), (1, 1), (0, 0)))

    def flatten_rows(values):
        return values.reshape(-1, channels)

    padded_in = padded_rows(frames_in)
    pre = jnp.zeros((slab_rows * width_cells, channels), jnp.float32)
    for tap_row in range(3):
        for tap_col in range(3):
            window = flatten_rows(
                padded_in[tap_row : tap_row + slab_rows, tap_col : tap_col + width_cells]
            )
            pre = pre + jnp.dot(
                window, spatial_weight[tap_row, tap_col], preferred_element_type=jnp.float32
            )
    act = jax.nn.silu(pre).astype(jnp.bfloat16).reshape(slab_rows, width_cells, channels)

    def to_frames(values):
        return lax.all_to_all(values, "sp", split_axis=0, concat_axis=1, tiled=True)

    moved_act, moved_cot = (
        lax.all_to_all(act, "sp", split_axis=1, concat_axis=0, tiled=True),
        lax.all_to_all(cotangent, "sp", split_axis=1, concat_axis=0, tiled=True),
    )
    group_rows = slab_rows * sp_count
    stripe = width_cells // sp_count
    groups = group_rows // (FRAMES * H)
    act_clips = moved_act.reshape(groups, FRAMES, H * stripe, channels)
    cot_clips = moved_cot.reshape(groups, FRAMES, H * stripe, channels)
    act_padded = jnp.pad(act_clips, ((0, 0), (2, 0), (0, 0), (0, 0)))
    cot_padded = jnp.pad(cot_clips, ((0, 0), (0, 2), (0, 0), (0, 0)))
    temporal_sum = jnp.zeros(act_clips.shape, jnp.float32)
    act_grad_sum = jnp.zeros(act_clips.shape, jnp.float32)
    temporal_terms = []
    for tap_step in range(3):
        earlier = act_padded[:, 2 - tap_step : 2 - tap_step + FRAMES]
        temporal_sum = temporal_sum + jnp.einsum(
            "gfpc,cd->gfpd", earlier, temporal_weight[tap_step], preferred_element_type=jnp.float32
        )
        temporal_terms.append(
            jnp.einsum("gfpc,gfpd->cd", earlier, cot_clips, preferred_element_type=jnp.float32)
        )
        later = cot_padded[:, tap_step : tap_step + FRAMES]
        act_grad_sum = act_grad_sum + jnp.einsum(
            "gfpd,cd->gfpc", later, temporal_weight[tap_step], preferred_element_type=jnp.float32
        )
    temporal_out = to_frames(
        temporal_sum.astype(jnp.bfloat16).reshape(group_rows, stripe, channels)
    )
    grad_act = to_frames(act_grad_sum.astype(jnp.bfloat16).reshape(group_rows, stripe, channels))
    grad_temporal = jnp.stack(temporal_terms)
    grad_scale = 1.0 / math.sqrt(slab_rows * sp_count * lax.axis_size("dp") * width_cells)
    block_out = (frames_in.astype(jnp.float32) + temporal_out.astype(jnp.float32)).astype(
        jnp.bfloat16
    )
    sigma = jax.nn.sigmoid(pre)
    grad_pre = (
        flatten_rows(grad_act).astype(jnp.float32) * (sigma * (1.0 + pre * (1.0 - sigma)))
    ).astype(jnp.bfloat16)
    grad_padded = padded_rows(grad_pre.reshape(slab_rows, width_cells, channels))
    spatial_terms = []
    grad_in = flatten_rows(cotangent).astype(jnp.float32)
    for tap_row in range(3):
        for tap_col in range(3):
            window = flatten_rows(
                padded_in[tap_row : tap_row + slab_rows, tap_col : tap_col + width_cells]
            )
            spatial_terms.append(contract_rows(window, grad_pre))
            back_window = flatten_rows(
                grad_padded[
                    2 - tap_row : 2 - tap_row + slab_rows, 2 - tap_col : 2 - tap_col + width_cells
                ]
            )
            grad_in = grad_in + times_transpose(back_window, spatial_weight[tap_row, tap_col])
    grad_spatial = jnp.stack(spatial_terms).reshape(3, 3, channels, channels)
    grad_spatial, grad_temporal = lax.psum((grad_spatial, grad_temporal), ("dp", "sp"))
    grad_input = grad_in.astype(jnp.bfloat16).reshape(slab_rows, width_cells, channels)
    return (block_out, grad_input, grad_spatial * grad_scale, grad_temporal * grad_scale)


def solution(mesh):
    placed = (P(("dp", "sp"), None, None), P(), P(), P(("dp", "sp"), None, None))
    return jax.shard_map(
        local,
        mesh=mesh,
        in_specs=placed,
        out_specs=(P(("dp", "sp"), None, None), P(("dp", "sp"), None, None), P(), P()),
        check_vma=False,
    )
```

profile of v0, /device:TPU:0, one launch (start us, length us, event | category | flops | bytes accessed | tf_op | source)
XLA Modules:
  0.0 385.7 jit_solution(17746489602125472998)
XLA Ops:
  7.2 4.1 %copy.32 = bf16[64,64,256]{2,0,1:T(8,128)(2,1)} copy(bf16[64,64,256]{2,1,0:T(8,128)(2,1)} %param.7) | data formatting | bytes 4194304 | tf_op args[3]
  11.3 7.4 %all-to-all-start.2 = ((bf16[64,64,256]{2,0,1:T(8,128)(2,1)}), bf16[64,64,256]{2,0,1:T(8,128)(2,1)}, u32[]{:S(2)}, u32[]{:S(2)}) async-start(bf16[64,64,256]{2,0,1:T(8,128)(2,1)} %copy.32), calls=%async_computation.2 | async-start | bytes 4194304 | tf_op jit(solution)/shard_map/all_to_all | solution.py:50
  18.7 9.8 %pad_slice_fusion.10 = (bf16[64,64,256]{2,1,0:T(8,128)(2,1)}, bf16[64,64,256]{2,1,0:T(8,128)(2,1)}, bf16[64,64,256]{2,1,0:T(8,128)(2,1)}, bf16[64,64,256]{2,1,0:...) fusion(bf16[64,64,256]{2,1,0:T(8,128)(2,1)S(1)} %copy-done.3), kind=kLoop, calls=%fused_computation.46 | loop fusion | bytes 18874368 | tf_op jit(solution)/shard_map/slice | solution.py:38
  28.4 38.6 %all-to-all-done.2 = bf16[64,64,256]{2,0,1:T(8,128)(2,1)} async-done(((bf16[64,64,256]{2,0,1:T(8,128)(2,1)}), bf16[64,64,256]{2,0,1:T(8,128)(2,1)}, u32[]{:S(2)}, u32[]{:S(2)}) %all-to-all-start.2) | async-done | bytes 2097184 | tf_op jit(solution)/shard_map/all_to_all | solution.py:50
  67.0 2.9 copy.33
  71.4 2.1 add_convert_fusion
  73.5 4.8 %all-to-all-start.3 = ((bf16[512,8,256]{2,1,0:T(8,128)(2,1)}), bf16[512,8,256]{2,1,0:T(8,128)(2,1)}, u32[]{:S(2)}, u32[]{:S(2)}) async-start(bf16[512,8,256]{2,1,0:T(8,128)(2,1)} %bitcast.239), calls=%async_computation.3 | async-start | bytes 4194304 | tf_op jit(solution)/shard_map/all_to_all | solution.py:46
  78.3 2.4 fusion.63
  89.4 2.7 convolution_add_fusion.10
  92.1 34.0 %all-to-all-done.3 = bf16[512,8,256]{2,1,0:T(8,128)(2,1)} async-done(((bf16[512,8,256]{2,1,0:T(8,128)(2,1)}), bf16[512,8,256]{2,1,0:T(8,128)(2,1)}, u32[]{:S(2)}, u32[]{:S(2)}) %all-to-all-start.3) | async-done | bytes 2097184 | tf_op jit(solution)/shard_map/all_to_all | solution.py:46
  126.1 2.0 convert_bitcast_fusion
  128.7 1.6 copy-done.23
  130.9 3.5 fusion.2
  134.4 2.5 copy.29
  137.0 4.9 %all-to-all-start = ((bf16[64,64,256]{2,0,1:T(8,128)(2,1)}), bf16[64,64,256]{2,0,1:T(8,128)(2,1)}, u32[]{:S(2)}, u32[]{:S(2)}) async-start(bf16[64,64,256]{2,0,1:T(8,128)(2,1)} %copy.29), calls=%async_computation | async-start | bytes 4194304 | tf_op jit(solution)/shard_map/all_to_all | solution.py:49
  141.9 3.1 fusion.35
  149.3 1.0 fusion.31
  156.4 1.4 copy-done.24
  157.8 10.4 %pad_slice_fusion.2 = (bf16[64,64,256]{2,1,0:T(8,128)(2,1)}, bf16[64,64,256]{2,1,0:T(8,128)(2,1)S(1)}, bf16[64,64,256]{2,1,0:T(8,128)(2,1)S(1)}, bf16[64,64,256]...) fusion(bf16[64,64,256]{2,1,0:T(8,128)(2,1)S(1)} %bitcast.256), kind=kLoop, calls=%fused_computation.38 | loop fusion | bytes 18874368 | tf_op jit(solution)/shard_map/slice | solution.py:97
  171.3 2.8 convolution_add_fusion.4
  174.1 15.5 %all-to-all-done = bf16[64,64,256]{2,0,1:T(8,128)(2,1)} async-done(((bf16[64,64,256]{2,0,1:T(8,128)(2,1)}), bf16[64,64,256]{2,0,1:T(8,128)(2,1)}, u32[]{:S(2)}, u32[]{:S(2)}) %all-to-all-start) | async-done | bytes 2097184 | tf_op jit(solution)/shard_map/all_to_all | solution.py:49
  189.6 3.0 copy.30
  195.1 2.0 add_convert_fusion.1
  197.1 4.4 %all-to-all-start.1 = ((bf16[512,8,256]{2,1,0:T(8,128)(2,1)}), bf16[512,8,256]{2,1,0:T(8,128)(2,1)}, u32[]{:S(2)}, u32[]{:S(2)}) async-start(bf16[512,8,256]{2,1,0:T(8,128)(2,1)} %bitcast.238), calls=%async_computation.1 | async-start | bytes 4194304 | tf_op jit(solution)/shard_map/all_to_all | solution.py:46
  202.0 1.3 copy-done.2
  204.8 0.9 pad_maximum_fusion
  205.8 3.7 convolution_add_fusion.3
  212.7 2.1 fusion
  214.8 154.8 %all-reduce.7.cloned.1.call-done = (f32[3,3,256,256]{3,2,1,0:T(8,128)}, f32[3,256,256]{2,1,0:T(8,128)}) async-done(((f32[3,3,256,256]{3,2,1,0:T(8,128)}, f32[3,256,256]{2,1,0:T(8,128)}), (f32[3,3,256,256]{3,2,1,0:T(8,128)}, f32[3,256,256]{2,1,0:T(8,128)})) %all-reduce.7.cloned.1.call-update) | async-done | bytes 3145744 | tf_op jit(solution)/shard_map/psum | solution.py:103
  369.6 2.1 broadcast_multiply_fusion.1
  371.6 3.4 broadcast_multiply_fusion
  375.1 3.6 fusion.1
  (86 shorter events, 32.4 us)
Async XLA Ops:
  11.2 7.4 %copy-start.3 = (bf16[64,64,256]{2,1,0:T(8,128)(2,1)S(1)}, bf16[64,64,256]{2,1,0:T(8,128)(2,1)}, u32[]{:S(2)}) copy-start(bf16[64,64,256]{2,1,0:T(8,128)(2,1)} %param.4) | copy-start | bytes 6291460
  11.3 55.8 %all-to-all-start.2 = ((bf16[64,64,256]{2,0,1:T(8,128)(2,1)}), bf16[64,64,256]{2,0,1:T(8,128)(2,1)}, u32[]{:S(2)}, u32[]{:S(2)}) async-start(bf16[64,64,256]{2,0,1:T(8,128)(2,1)} %copy.32), calls=%async_computation.2 | async-start | bytes 4194304 | tf_op jit(solution)/shard_map/all_to_all | solution.py:50
  67.0 2.9 copy-start.27
  69.9 1.5 copy-start
  73.5 4.8 %copy-start.22 = (bf16[3,3,256,256]{3,2,1,0:T(8,128)(2,1)S(1)}, bf16[3,3,256,256]{3,2,1,0:T(8,128)(2,1)}, u32[]{:S(2)}) copy-start(bf16[3,3,256,256]{3,2,1,0:T(8,128)(2,1)} %param.5) | copy-start | bytes 3538948
  73.5 52.6 %all-to-all-start.3 = ((bf16[512,8,256]{2,1,0:T(8,128)(2,1)}), bf16[512,8,256]{2,1,0:T(8,128)(2,1)}, u32[]{:S(2)}, u32[]{:S(2)}) async-start(bf16[512,8,256]{2,1,0:T(8,128)(2,1)} %bitcast.239), calls=%async_computation.3 | async-start | bytes 4194304 | tf_op jit(solution)/shard_map/all_to_all | solution.py:46
  78.3 2.5 copy-start.19
  80.8 1.6 copy-start.16
  82.4 1.6 copy-start.13
  84.7 1.6 copy-start.10
  86.3 1.6 copy-start.8
  87.8 1.6 copy-start.6
  128.1 2.2 copy-start.23
  128.1 2.9 copy-start.25
  137.0 52.7 %all-to-all-start = ((bf16[64,64,256]{2,0,1:T(8,128)(2,1)}), bf16[64,64,256]{2,0,1:T(8,128)(2,1)}, u32[]{:S(2)}, u32[]{:S(2)}) async-start(bf16[64,64,256]{2,0,1:T(8,128)(2,1)} %copy.29), calls=%async_computation | async-start | bytes 4194304 | tf_op jit(solution)/shard_map/all_to_all | solution.py:49
  141.9 3.1 copy-start.20
  141.9 3.5 copy-start.21
  145.3 1.6 copy-start.17
  146.9 1.6 copy-start.14
  149.3 1.6 copy-start.11
  150.9 1.6 copy-start.9
  152.5 1.6 copy-start.7
  154.1 1.6 copy-start.26
  157.8 10.5 %copy-start.5 = (bf16[64,64,256]{2,1,0:T(8,128)(2,1)S(1)}, bf16[64,64,256]{2,1,0:T(8,128)(2,1)}, u32[]{:S(2)}) copy-start(bf16[64,64,256]{2,1,0:T(8,128)(2,1)} %param.7) | copy-start | bytes 6291460
  189.6 3.0 copy-start.1
  197.1 178.0 %all-to-all-start.1 = ((bf16[512,8,256]{2,1,0:T(8,128)(2,1)}), bf16[512,8,256]{2,1,0:T(8,128)(2,1)}, u32[]{:S(2)}, u32[]{:S(2)}) async-start(bf16[512,8,256]{2,1,0:T(8,128)(2,1)} %bitcast.238), calls=%async_computation.1 | async-start | bytes 4194304 | tf_op jit(solution)/shard_map/all_to_all | solution.py:46
  201.5 168.1 %all-reduce.7.cloned.1.call-start = ((), (), s32[]{:S(2)}) async-start(), calls=%async_computation.4 | async-start | bytes 6291456 | tf_op jit(solution)/shard_map/psum | solution.py:103
  201.7 1.6 copy-start.2
  205.8 3.7 copy-start.18
  209.5 1.6 copy-start.15
  211.1 1.6 copy-start.12
  371.6 3.4 copy-start.4
  (2 other events, 2.4 us)
Sparse Core Ops, SparseCore 0:
  208.5 160.9 all-reduce.6
where the time goes:
time: 393 us; the launch traced here: 386 us
  waiting for transfers between devices  243 us (62%)
  local copies, waits for them, and re-layouts  49.7 us (13%)
  matrix products  44.8 us (11%)
  starting transfers between devices  21.7 us (6%)
  between operations  14.7 us (4%)
  other arithmetic  12 us (3%)
    psum x1, waiting for transfers between devices, local(): lax.psum((grad_spatial, grad_temporal), ('dp', 'sp'))  155 us
    all_to_all x1, waiting for transfers between devices, local(): lax.all_to_all(cotangent, 'sp', split_axis=1, concat_axis=0, tiled=True)  38.6 us
    all_to_all x2, waiting for transfers between devices, to_frames(): return lax.all_to_all(values, 'sp', split_axis=0, concat_axis=1, tiled=True)  34 us
    unnamed x59, local copies, waits for them, and re-layouts  20.2 us
    all_to_all x1, waiting for transfers between devices, local(): lax.all_to_all(act, 'sp', split_axis=1, concat_axis=0, tiled=True)  15.5 us
    dot_general x9, matrix products, times_transpose(): lax.dot_general(left, weight, (((1,), (1,)), ((), ())), preferred_element...  13.1 us
    dot_general x9, matrix products, local(): jnp.dot(window, spatial_weight[tap_row, tap_col], preferred_element_type=...  13 us
    slice x1, local copies, waits for them, and re-layouts, local(): grad_padded[2 - tap_row:2 - tap_row + slab_rows, 2 - tap_col:2 - tap_col...  10.4 us
  transfers between devices with their start and end apart: 5, of which 4 were waited for; matrix products, arithmetic and copies ran while one was open for 16% of the time, Pallas kernels for 0%

commit v1 on v0

--- a/solution.py
+++ b/solution.py
@@ -21,6 +21,19 @@
 
 
 def local(frames_in, spatial_weight, temporal_weight, cotangent):
+
+    def supply_all_outputs(x0, named_axis):
+        met_up = jnp.concatenate(
+            jax.lax.all_to_all(
+                jnp.stack(jnp.split(x0, jax.lax.psum(1, axis_name=named_axis), axis=1)),
+                concat_axis=0,
+                split_axis=0,
+                axis_name=named_axis,
+            ),
+            axis=0,
+        )
+        return met_up
+
     slab_rows, width_cells, channels = frames_in.shape
     sp_count = lax.axis_size("sp")
 
@@ -47,7 +60,7 @@
 
     moved_act, moved_cot = (
         lax.all_to_all(act, "sp", split_axis=1, concat_axis=0, tiled=True),
-        lax.all_to_all(cotangent, "sp", split_axis=1, concat_axis=0, tiled=True),
+        supply_all_outputs(cotangent, "sp"),
     )
     group_rows = slab_rows * sp_count
     stripe = width_cells // sp_count

time: 393 us -> 392 us (level); the launches traced: 386 us -> 391 us
  local copies, waits for them, and re-layouts: 49.7 us -> 62.1 us
  waiting for transfers between devices: 243 us -> 239 us
    unnamed x59 -> x69, local copies, waits for them, and re-layouts: 20.2 us -> 30.4 us
where the time goes in v1:
time: 392 us; the launch traced here: 391 us
  waiting for transfers between devices  239 us (61%)
  local copies, waits for them, and re-layouts  62.1 us (16%)
  matrix products  42.3 us (11%)
  starting transfers between devices  21.4 us (5%)
  between operations  14.4 us (4%)
  other arithmetic  11.9 us (3%)
    psum x1, waiting for transfers between devices, local(): lax.psum((grad_spatial, grad_temporal), ('dp', 'sp'))  154 us
    all_to_all x1, waiting for transfers between devices, supply_all_outputs(): jax.lax.all_to_all(jnp.stack(jnp.split(x0, jax.lax.psum(1, axis_name=name...  35 us
    all_to_all x2, waiting for transfers between devices, to_frames(): return lax.all_to_all(values, 'sp', split_axis=0, concat_axis=1, tiled=True)  33.9 us
    unnamed x69, local copies, waits for them, and re-layouts  30.4 us
    all_to_all x1, waiting for transfers between devices, local(): lax.all_to_all(act, 'sp', split_axis=1, concat_axis=0, tiled=True)  15.6 us
    slice x1, local copies, waits for them, and re-layouts, local(): padded_in[tap_row:tap_row + slab_rows, tap_col:tap_col + width_cells]  13.2 us
    dot_general x9, matrix products, times_transpose(): lax.dot_general(left, weight, (((1,), (1,)), ((), ())), preferred_element...  12.4 us
    dot_general x9, matrix products, local(): jnp.dot(window, spatial_weight[tap_row, tap_col], preferred_element_type=...  11.2 us
  transfers between devices with their start and end apart: 5, of which 4 were waited for; matrix products, arithmetic and copies ran while one was open for 16% of the time, Pallas kernels for 0%

profile of v1, /device:TPU:0, one launch (start us, length us, event | category | flops | bytes accessed | tf_op | source)
XLA Modules:
  0.0 390.6 jit_solution(12950314654318129451)
XLA Ops:
  7.2 1.7 bitcast_dynamic-update-slice_fusion.7
  8.8 1.7 bitcast_dynamic-update-slice_fusion.6
  10.5 1.7 bitcast_dynamic-update-slice_fusion.5
  12.2 1.7 bitcast_dynamic-update-slice_fusion.4
  13.8 1.7 bitcast_dynamic-update-slice_fusion.3
  15.5 1.7 bitcast_dynamic-update-slice_fusion.2
  17.2 1.7 bitcast_dynamic-update-slice_fusion.1
  18.8 1.7 bitcast_dynamic-update-slice_fusion
  20.5 7.3 %all-to-all-start.2 = ((bf16[8,64,8,256]{3,2,1,0:T(8,128)(2,1)}), bf16[8,64,8,256]{3,2,1,0:T(8,128)(2,1)S(1)}, u32[]{:S(2)}, u32[]{:S(2)}) async-start(bf16[8,64,8,256]{3,2,1,0:T(8,128)(2,1)} %bitcast_dynamic-update-slice_fusion), calls=%async_computation.2 | async-start | bytes 4194304 | tf_op jit(solution)/shard_map/all_to_all | solution.py:27
  27.8 13.2 %pad_slice_fusion.10 = (bf16[64,64,256]{2,1,0:T(8,128)(2,1)}, bf16[64,64,256]{2,1,0:T(8,128)(2,1)}, bf16[64,64,256]{2,1,0:T(8,128)(2,1)}, bf16[64,64,256]{2,1,0:...) fusion(bf16[64,64,256]{2,1,0:T(8,128)(2,1)} %param.4), kind=kLoop, calls=%fused_computation.46 | loop fusion | bytes 18874368 | tf_op jit(solution)/shard_map/slice | solution.py:51
  41.1 35.0 %all-to-all-done.2 = bf16[8,64,8,256]{3,2,1,0:T(8,128)(2,1)S(1)} async-done(((bf16[8,64,8,256]{3,2,1,0:T(8,128)(2,1)}), bf16[8,64,8,256]{3,2,1,0:T(8,128)(2,1)S(1)}, u32[]{:S(2)}, u32[]{:S(2)}) %all-to-all-start.2) | async-done | bytes 2097184 | tf_op jit(solution)/shard_map/all_to_all | solution.py:27
  77.5 2.1 add_convert_fusion
  79.6 4.8 %all-to-all-start.3 = ((bf16[512,8,256]{2,1,0:T(8,128)(2,1)}), bf16[512,8,256]{2,1,0:T(8,128)(2,1)}, u32[]{:S(2)}, u32[]{:S(2)}) async-start(bf16[512,8,256]{2,1,0:T(8,128)(2,1)} %bitcast.252), calls=%async_computation.3 | async-start | bytes 4194304 | tf_op jit(solution)/shard_map/all_to_all | solution.py:59
  95.6 2.7 convolution_add_fusion.10
  98.3 33.9 %all-to-all-done.3 = bf16[512,8,256]{2,1,0:T(8,128)(2,1)} async-done(((bf16[512,8,256]{2,1,0:T(8,128)(2,1)}), bf16[512,8,256]{2,1,0:T(8,128)(2,1)}, u32[]{:S(2)}, u32[]{:S(2)}) %all-to-all-start.3) | async-done | bytes 2097184 | tf_op jit(solution)/shard_map/all_to_all | solution.py:59
  132.1 2.0 convert_bitcast_fusion
  137.0 3.5 fusion.2
  140.4 2.5 copy.27
  143.0 4.6 %all-to-all-start = ((bf16[64,64,256]{2,0,1:T(8,128)(2,1)}), bf16[64,64,256]{2,0,1:T(8,128)(2,1)}, u32[]{:S(2)}, u32[]{:S(2)}) async-start(bf16[64,64,256]{2,0,1:T(8,128)(2,1)} %copy.27), calls=%async_computation | async-start | bytes 4194304 | tf_op jit(solution)/shard_map/all_to_all | solution.py:62
  147.6 3.1 fusion.35
  163.5 10.3 %pad_slice_fusion.2 = (bf16[64,64,256]{2,1,0:T(8,128)(2,1)}, bf16[64,64,256]{2,1,0:T(8,128)(2,1)S(1)}, bf16[64,64,256]{2,1,0:T(8,128)(2,1)S(1)}, bf16[64,64,256]...) fusion(bf16[64,64,256]{2,1,0:T(8,128)(2,1)S(1)} %bitcast.269), kind=kLoop, calls=%fused_computation.38 | loop fusion | bytes 18874368 | tf_op jit(solution)/shard_map/slice | solution.py:110
  176.8 2.8 convolution_add_fusion.4
  179.6 15.6 %all-to-all-done = bf16[64,64,256]{2,0,1:T(8,128)(2,1)} async-done(((bf16[64,64,256]{2,0,1:T(8,128)(2,1)}), bf16[64,64,256]{2,0,1:T(8,128)(2,1)}, u32[]{:S(2)}, u32[]{:S(2)}) %all-to-all-start) | async-done | bytes 2097184 | tf_op jit(solution)/shard_map/all_to_all | solution.py:62
  195.2 3.0 copy.28
  200.6 2.0 add_convert_fusion.1
  202.6 4.4 %all-to-all-start.1 = ((bf16[512,8,256]{2,1,0:T(8,128)(2,1)}), bf16[512,8,256]{2,1,0:T(8,128)(2,1)}, u32[]{:S(2)}, u32[]{:S(2)}) async-start(bf16[512,8,256]{2,1,0:T(8,128)(2,1)} %bitcast.251), calls=%async_computation.1 | async-start | bytes 4194304 | tf_op jit(solution)/shard_map/all_to_all | solution.py:59
  212.3 3.1 convolution_add_fusion.3
  218.6 2.1 fusion
  220.6 154.1 %all-reduce.7.cloned.1.call-done = (f32[3,3,256,256]{3,2,1,0:T(8,128)}, f32[3,256,256]{2,1,0:T(8,128)}) async-done(((f32[3,3,256,256]{3,2,1,0:T(8,128)}, f32[3,256,256]{2,1,0:T(8,128)}), (f32[3,3,256,256]{3,2,1,0:T(8,128)}, f32[3,256,256]{2,1,0:T(8,128)})) %all-reduce.7.cloned.1.call-update) | async-done | bytes 3145744 | tf_op jit(solution)/shard_map/psum | solution.py:116
  374.8 2.1 broadcast_multiply_fusion.1
  376.9 3.4 broadcast_multiply_fusion
  380.3 3.5 fusion.1
  (96 shorter events, 41.9 us)
Async XLA Ops:
  20.5 55.5 %all-to-all-start.2 = ((bf16[8,64,8,256]{3,2,1,0:T(8,128)(2,1)}), bf16[8,64,8,256]{3,2,1,0:T(8,128)(2,1)S(1)}, u32[]{:S(2)}, u32[]{:S(2)}) async-start(bf16[8,64,8,256]{3,2,1,0:T(8,128)(2,1)} %bitcast_dynamic-update-slice_fusion), calls=%async_computation.2 | async-start | bytes 4194304 | tf_op jit(solution)/shard_map/all_to_all | solution.py:27
  27.8 48.2 %copy-start.29 = (bf16[3,256,256]{2,1,0:T(8,128)(2,1)S(1)}, bf16[3,256,256]{2,1,0:T(8,128)(2,1)}, u32[]{:S(2)}) copy-start(bf16[3,256,256]{2,1,0:T(8,128)(2,1)} %param.6) | copy-start | bytes 1179652
  79.6 4.8 %copy-start.6 = (bf16[64,64,256]{2,1,0:T(8,128)(2,1)S(1)}, bf16[64,64,256]{2,1,0:T(8,128)(2,1)}, u32[]{:S(2)}) copy-start(bf16[64,64,256]{2,1,0:T(8,128)(2,1)} %get-tuple-element.25) | copy-start | bytes 6291460
  79.6 4.8 %copy-start.24 = (bf16[3,3,256,256]{3,2,1,0:T(8,128)(2,1)S(1)}, bf16[3,3,256,256]{3,2,1,0:T(8,128)(2,1)}, u32[]{:S(2)}) copy-start(bf16[3,3,256,256]{3,2,1,0:T(8,128)(2,1)} %param.5) | copy-start | bytes 3538948
  79.6 52.5 %all-to-all-start.3 = ((bf16[512,8,256]{2,1,0:T(8,128)(2,1)}), bf16[512,8,256]{2,1,0:T(8,128)(2,1)}, u32[]{:S(2)}, u32[]{:S(2)}) async-start(bf16[512,8,256]{2,1,0:T(8,128)(2,1)} %bitcast.252), calls=%async_computation.3 | async-start | bytes 4194304 | tf_op jit(solution)/shard_map/all_to_all | solution.py:59
  84.4 1.6 copy-start.21
  86.0 1.6 copy-start.18
  87.6 1.6 copy-start.15
  89.2 1.6 copy-start.3
  90.8 1.6 copy-start.11
  92.4 1.6 copy-start.9
  94.0 1.6 copy-start.7
  134.1 2.2 copy-start.25
  134.1 2.9 copy-start.27
  143.0 52.2 %all-to-all-start = ((bf16[64,64,256]{2,0,1:T(8,128)(2,1)}), bf16[64,64,256]{2,0,1:T(8,128)(2,1)}, u32[]{:S(2)}, u32[]{:S(2)}) async-start(bf16[64,64,256]{2,0,1:T(8,128)(2,1)} %copy.27), calls=%async_computation | async-start | bytes 4194304 | tf_op jit(solution)/shard_map/all_to_all | solution.py:62
  147.6 3.1 copy-start.22
  147.6 3.5 copy-start.23
  151.0 1.6 copy-start.19
  152.6 1.6 copy-start.16
  155.0 1.6 copy-start.12
  156.6 1.6 copy-start.10
  158.2 1.6 copy-start.8
  159.8 1.6 copy-start.28
  163.5 10.3 %copy-start.5 = (bf16[64,64,256]{2,1,0:T(8,128)(2,1)S(1)}, bf16[64,64,256]{2,1,0:T(8,128)(2,1)}, u32[]{:S(2)}) copy-start(bf16[64,64,256]{2,1,0:T(8,128)(2,1)} %param.7) | copy-start | bytes 6291460
  195.2 3.0 copy-start.1
  202.6 177.7 %all-to-all-start.1 = ((bf16[512,8,256]{2,1,0:T(8,128)(2,1)}), bf16[512,8,256]{2,1,0:T(8,128)(2,1)}, u32[]{:S(2)}, u32[]{:S(2)}) async-start(bf16[512,8,256]{2,1,0:T(8,128)(2,1)} %bitcast.251), calls=%async_computation.1 | async-start | bytes 4194304 | tf_op jit(solution)/shard_map/all_to_all | solution.py:59
  207.0 167.8 %all-reduce.7.cloned.1.call-start = ((), (), s32[]{:S(2)}) async-start(), calls=%async_computation.4 | async-start | bytes 6291456 | tf_op jit(solution)/shard_map/psum | solution.py:116
  207.3 1.6 copy-start.2
  210.4 1.9 copy-start.20
  212.3 3.1 copy-start.17
  215.4 1.6 copy-start.14
  376.9 3.4 copy-start.4
  (4 other events, 5.5 us)
Sparse Core Ops, SparseCore 0:
  214.0 160.7 all-reduce.6
